TPU v7x, 512 devices: a whole 4x8x8 slice. The times are simulated.
512 devices in a mesh: dp: 2 (over core), row: 16 (over z, x_hi), col: 16 (over x_lo, y).
Axes of the slice: x: 4 (x_hi: 2, x_lo: 2; x = x_hi * 2 + x_lo), y: 8, z: 8, core: 2. Of those that a mesh axis runs over, the one named last changes fastest.
Arguments:
- tokens: bfloat16 [512, 12288], P(('dp', 'col'), 'row'), may hold values from -6 to 6
- w_up: bfloat16 [12288, 24576], P('row', ('dp', 'col')), may hold values from -0.0546875 to 0.0546875
- w_down: bfloat16 [24576, 12288], P(('dp', 'col'), 'row'), may hold values from -0.0390625 to 0.0390625
- grad_out: bfloat16 [512, 12288], P(('dp', 'col'), 'row'), may hold values from -6 to 6
Outputs:
- grad_tokens: bfloat16 [512, 12288], P(('dp', 'col'), 'row')
- grad_w_up: bfloat16 [12288, 24576], P('row', ('dp', 'col'))
- grad_w_down: bfloat16 [24576, 12288], P(('dp', 'col'), 'row')
All inputs are finite; a program needn't handle non-finite values.
Results may differ from a plain program's by a relative error of at most 0.0049.
Values may be sent and summed in bfloat16 or wider, within the bound.
A program may use at most 64 MiB of HBM per device.

v0:
```python
import math

import jax
import jax.numpy as jnp
from jax import lax
from jax.sharding import PartitionSpec as P

slope_c = math.sqrt(2.0 / math.pi)
cubic_a = 0.044715


def gelu_value(u):
    t = jnp.tanh(slope_c * (u + cubic_a * u * u * u))
    return 0.5 * u * (1.0 + t)


def gelu_slope(u):
    t = jnp.tanh(slope_c * (u + cubic_a * u * u * u))
    return 0.5 * (1.0 + t) + 0.5 * u * (1.0 - t * t) * slope_c * (1.0 + 3.0 * cubic_a * u * u)


def outer_rows(left, right):
    return lax.dot_general(
        left, right, (((0,), (0,)), ((), ())), preferred_element_type=jnp.float32
    )


def times_transposed(left, right):
    return lax.dot_general(
        left, right, (((1,), (1,)), ((), ())), preferred_element_type=jnp.float32
    )


def per_device(tokens, w_up, w_down, grad_out):
    full_x, full_dy = (
        lax.all_gather(tokens, ("dp", "col"), axis=0, tiled=True),
        lax.all_gather(grad_out, ("dp", "col"), axis=0, tiled=True),
    )
    block = full_x
    pre = lax.psum_scatter(
        jnp.dot(block, w_up, preferred_element_type=jnp.float32),
        "row",
        scatter_dimension=0,
        tiled=True,
    )
    act = gelu_value(pre).astype(jnp.bfloat16)
    grad_down = outer_rows(lax.all_gather(act, "row", axis=0, tiled=True), full_dy)
    block = full_dy
    grad_act = lax.psum_scatter(
        times_transposed(block, w_down), "row", scatter_dimension=0, tiled=True
    )
    grad_pre_rows = (grad_act * gelu_slope(pre)).astype(jnp.bfloat16)
    grad_pre = lax.all_gather(grad_pre_rows, "row", axis=0, tiled=True)
    grad_up = outer_rows(full_x, grad_pre)
    block = grad_pre
    grad_in = lax.psum_scatter(
        times_transposed(block, w_up), ("dp", "col"), scatter_dimension=0, tiled=True
    )
    return (
        grad_in.astype(jnp.bfloat16),
        grad_up.astype(jnp.bfloat16),
        grad_down.astype(jnp.bfloat16),
    )


def solution(mesh):
    in_specs = (
        P(("dp", "col"), "row"),
        P("row", ("dp", "col")),
        P(("dp", "col"), "row"),
        P(("dp", "col"), "row"),
    )
    out_specs = (P(("dp", "col"), "row"), P("row", ("dp", "col")), P(("dp", "col"), "row"))
    return jax.shard_map(
        per_device, mesh=mesh, in_specs=in_specs, out_specs=out_specs, check_vma=False
    )
```

profile of v0, /device:TPU:6, one launch (start us, length us, event | category | flops | bytes accessed | tf_op | source)
XLA Modules:
  0.0 687.1 jit_solution(7192536462443622004)
XLA Ops:
  7.2 0.0 copy-start
  7.2 0.0 reduce-scatter.6.cloned.1.call-start
  7.2 66.9 %all_gather.13 = bf16[512,768]{1,0:T(8,128)(2,1)S(1)} all-gather(bf16[16,768]{1,0:T(8,128)(2,1)} %param.4), channel_id=1, replica_groups=mesh['dp'=2,'row'=16,'col'=16] {'dp','col'}, dimensions={0}, use_global_device_ids=true | all-gather | bytes 811008 | tf_op jit(solution)/shard_map/all_gather | solution.py:36
  74.2 0.0 copy-done
  74.2 1.9 fusion.9
  76.1 0.0 copy-start.4
  76.1 0.0 reduce-scatter.6.cloned.1.call-update
  76.1 0.0 reduce-scatter.4.cloned.1.call-start
  76.2 0.7 copy-done.4
  76.8 62.6 %all_gather.12 = bf16[512,768]{1,0:T(8,128)(2,1)S(1)} all-gather(bf16[16,768]{1,0:T(8,128)(2,1)S(1)} %copy-done.4), channel_id=1, replica_groups=mesh['dp'=2,'row'=16,'col'=16] {'dp','col'}, dimensions={0}, use_global_device_ids=true | all-gather | bytes 811008 | tf_op jit(solution)/shard_map/all_gather | solution.py:37
  139.4 0.0 copy-start.1
  139.4 3.5 fusion.8
  142.9 0.0 copy-done.1
  142.9 0.0 reduce-scatter.4.cloned.1.call-update
  143.0 0.0 reduce-scatter.8.cloned.1.call-start
  143.0 142.9 %reduce-scatter.6.cloned.1.call-done = f32[32,768]{1,0:T(8,128)} async-done(((f32[512,768]{1,0:T(8,128)}), f32[32,768]{1,0:T(8,128)}) %reduce-scatter.6.cloned.1.call-update) | async-done | bytes 98320 | tf_op jit(solution)/shard_map/reduce_scatter | solution.py:40
  285.9 214.1 %reduce-scatter.4.cloned.1.call-done = f32[32,768]{1,0:T(8,128)} async-done(((f32[512,768]{1,0:T(8,128)}), f32[32,768]{1,0:T(8,128)}) %reduce-scatter.4.cloned.1.call-update) | async-done | bytes 98320 | tf_op jit(solution)/shard_map/reduce_scatter | solution.py:49
  500.0 1.0 multiply_convert_fusion
  501.0 42.5 %all_gather.14 = bf16[512,768]{1,0:T(8,128)(2,1)S(1)} all-gather(bf16[32,768]{1,0:T(8,128)(2,1)S(1)} %get-tuple-element.7), channel_id=1, replica_groups=mesh['dp'=2,'row'=16,'col'=16] {'row'}, dimensions={0}, use_global_device_ids=true | all-gather | bytes 835584 | tf_op jit(solution)/shard_map/all_gather | solution.py:53
  543.5 0.0 copy-start.3
  543.5 0.9 copy-done.3
  544.4 2.0 fusion.10
  546.4 0.0 reduce-scatter.8.cloned.1.call-update
  546.4 1.9 fusion
  548.3 0.0 copy-start.2
  548.4 1.5 copy.7
  549.8 42.7 %all_gather.15 = bf16[512,768]{1,0:T(8,128)(2,1)S(1)} all-gather(bf16[32,768]{1,0:T(8,128)(2,1)S(1)} %get-tuple-element.6), channel_id=1, replica_groups=mesh['dp'=2,'row'=16,'col'=16] {'row'}, dimensions={0}, use_global_device_ids=true | all-gather | bytes 835584 | tf_op jit(solution)/shard_map/all_gather | solution.py:47
  592.5 0.0 copy-done.2
  592.5 1.8 convolution_convert_fusion
  594.4 84.8 %reduce-scatter.8.cloned.1.call-done = f32[16,768]{1,0:T(8,128)} async-done(((f32[512,768]{1,0:T(8,128)}), f32[16,768]{1,0:T(8,128)}) %reduce-scatter.8.cloned.1.call-update) | async-done | bytes 49168 | tf_op jit(solution)/shard_map/reduce_scatter | solution.py:56
  679.2 1.4 convert_element_type.19
Async XLA Ops:
  7.2 67.0 %copy-start = (bf16[768,768]{1,0:T(8,128)(2,1)S(1)}, bf16[768,768]{1,0:T(8,128)(2,1)}, u32[]{:S(2)}) copy-start(bf16[768,768]{1,0:T(8,128)(2,1)} %param.5) | copy-start | bytes 3538948
  7.2 278.7 %reduce-scatter.6.cloned.1.call-start = ((), (), s32[]{:S(2)}) async-start(), calls=%async_computation.4 | async-start | bytes 1671168 | tf_op jit(solution)/shard_map/reduce_scatter | solution.py:40
  76.1 0.7 copy-start.4
  76.1 423.9 %reduce-scatter.4.cloned.1.call-start = ((), (), s32[]{:S(2)}) async-start(), calls=%async_computation.3 | async-start | bytes 1671168 | tf_op jit(solution)/shard_map/reduce_scatter | solution.py:49
  139.4 3.5 copy-start.1
  143.0 536.2 %reduce-scatter.8.cloned.1.call-start = ((), (), s32[]{:S(2)}) async-start(), calls=%async_computation.5 | async-start | bytes 1622016 | tf_op jit(solution)/shard_map/reduce_scatter | solution.py:56
  543.5 0.9 copy-start.3
  548.3 44.2 %copy-start.2 = (bf16[512,768]{1,0:T(8,128)(2,1)S(1)}, bf16[512,768]{1,0:T(8,128)(2,1)}, u32[]{:S(2)}) copy-start(bf16[512,768]{1,0:T(8,128)(2,1)} %copy-done.1) | copy-start | bytes 2359300
Sparse Core Ops, SparseCore 0:
  76.2 209.6 reduce-scatter.5
  291.0 208.9 reduce-scatter.3
  546.5 132.6 reduce-scatter.7
where the time goes:
time: 687 us
  waiting for transfers between devices  442 us (64%)
  blocking collectives  215 us (31%)
  between operations  13.8 us (2%)
  matrix products  11.2 us (2%)
    reduce_scatter x1, waiting for transfers between devices, per_device(): lax.psum_scatter(times_transposed(block, w_down), 'row', scatter_dimensio...  214 us
    reduce_scatter x1, waiting for transfers between devices, per_device(): lax.psum_scatter(jnp.dot(block, w_up, preferred_element_type=jnp.float32)...  143 us
    reduce_scatter x1, waiting for transfers between devices, per_device(): lax.psum_scatter(times_transposed(block, w_up), ('dp', 'col'), scatter_di...  84.8 us
    all_gather x1, blocking collectives, per_device(): lax.all_gather(tokens, ('dp', 'col'), axis=0, tiled=True)  66.9 us
    all_gather x1, blocking collectives, per_device(): lax.all_gather(grad_out, ('dp', 'col'), axis=0, tiled=True)  62.6 us
    all_gather x1, blocking collectives, per_device(): lax.all_gather(act, 'row', axis=0, tiled=True)  42.7 us
    all_gather x1, blocking collectives, per_device(): grad_pre = lax.all_gather(grad_pre_rows, 'row', axis=0, tiled=True)  42.5 us
  transfers between devices with their start and end apart: 3, of which 3 were waited for; matrix products, arithmetic and copies ran while one was open for 1% of the time, Pallas kernels for 0%

commit v1 on v0

v1 whole, which is shorter than its diff:
```python
import functools
import math

import jax
import jax.numpy as jnp
from jax import lax
from jax.experimental import pallas as pl
from jax.experimental.pallas import tpu as pltpu
from jax.sharding import PartitionSpec as P

slope_c = math.sqrt(2.0 / math.pi)
cubic_a = 0.044715
f32 = jnp.float32
bf16 = jnp.bfloat16
tile = 16


def dot_plain(left, right):
    return lax.dot_general(left, right, (((1,), (0,)), ((), ())), preferred_element_type=f32)


def dot_right_t(left, right):
    return lax.dot_general(left, right, (((1,), (1,)), ((), ())), preferred_element_type=f32)


def dot_left_t(left, right):
    return lax.dot_general(left, right, (((0,), (0,)), ((), ())), preferred_element_type=f32)


def remote(src, dst, send_sem, recv_sem, device):
    return pltpu.make_async_remote_copy(
        src_ref=src,
        dst_ref=dst,
        send_sem=send_sem,
        recv_sem=recv_sem,
        device_id=device,
        device_id_type=pl.DeviceIdType.MESH,
    )


class Ring:
    def __init__(self, place, size, up, down, ups, downs, send_sems, recv_sems, sent):
        self.place, self.size, self.sent = place, size, sent
        self.ways = ((1, ups, 0, up), (-1, downs, ups, down))
        self.send_sems, self.recv_sems = send_sems, recv_sems

    def at(self, offset):
        return lax.rem(self.place + (offset + self.size), self.size)


class Gather(Ring):
    def copy(self, way, step, view, received=False):
        sign, _, base, device = way
        q = self.at(-sign * (step + 1 if received else step))
        ref = view(q)
        slot = base + step
        return remote(ref, ref, self.send_sems.at[slot], self.recv_sems.at[slot], device)

    def send(self, step, view):
        for way in self.ways:
            if step < way[1]:
                copy = self.copy(way, step, view)
                copy.start()
                self.sent.append(copy)

    def arrive(self, step, view):
        here = []
        for way in self.ways:
            if step < way[1]:
                self.copy(way, step, view, received=True).wait_recv()
                here.append(self.at(-way[0] * (step + 1)))
        return here


class Scatter(Ring):
    def bind(self, part, out_slots, in_slots):
        self.part, self.out_slots, self.in_slots = part, out_slots, in_slots
        return self

    def copy(self, way, step):
        _, _, base, device = way
        slot = base + step
        return remote(
            self.out_slots.at[slot],
            self.in_slots.at[slot],
            self.send_sems.at[slot],
            self.recv_sems.at[slot],
            device,
        )

    def step(self, step):
        for way in self.ways:
            sign, hops, base, _ = way
            if step < hops:
                total = self.part(self.at(sign * (hops - step)))
                if step > 0:
                    self.copy(way, step - 1).wait_recv()
                    total = total + self.in_slots[base + step - 1].astype(f32)
                self.out_slots[base + step] = total.astype(self.out_slots.dtype)
                copy = self.copy(way, step)
                copy.start()
                self.sent.append(copy)

    def finish(self):
        total = self.part(self.place)
        for way in self.ways:
            _, hops, base, _ = way
            if hops > 0:
                self.copy(way, hops - 1).wait_recv()
                total = total + self.in_slots[base + hops - 1].astype(f32)
        return total


def kernel(
    nz, ny,
    x_in, wu_in, wd_in, dy_in,
    gin_out, gu_out, gd_out,
    xg, dyg, wu, wd, pre_p, gact_p,
    pre_out, pre_in, gact_out, gact_in,
    pair_out, pair_in, slope,
    act, gpre, gin_p, sib_out, sib_in, gin_o, gin_i, last_out, last_in, gu, gd,
    local_sem, xlo_s, xlo_r, y_s, y_r, sib_s, sib_r, z_s, z_r, pair_s, pair_r,
    gsib_s, gsib_r, gy_s, gy_r, gx_s, gx_r,
):
    core = lax.axis_index("dp")
    row = lax.axis_index("row")
    col = lax.axis_index("col")
    z, x_hi = lax.div(row, 2), lax.rem(row, 2)
    x_lo, y = lax.div(col, ny), lax.rem(col, ny)
    sent = []

    def start(copy):
        copy.start()
        sent.append(copy)

    z_up = {"row": lax.rem(z + 1, nz) * 2 + x_hi}
    z_down = {"row": lax.rem(z + nz - 1, nz) * 2 + x_hi}
    far = {"row": z * 2 + (1 - x_hi)}
    y_up = {"col": x_lo * ny + lax.rem(y + 1, ny)}
    y_down = {"col": x_lo * ny + lax.rem(y + ny - 1, ny)}
    near = {"col": (1 - x_lo) * ny + y}
    sibling = {"dp": 1 - core}

    mine = pl.ds(pl.multiple_of(core * (2 * tile), 2 * tile), 2 * tile)
    theirs = pl.ds(pl.multiple_of((1 - core) * (2 * tile), 2 * tile), 2 * tile)
    own_tile = pl.ds(pl.multiple_of(core * (2 * tile) + x_lo * tile, tile), tile)
    near_tile = pl.ds(pl.multiple_of(core * (2 * tile) + (1 - x_lo) * tile, tile), tile)

    fetch_x = pltpu.make_async_copy(x_in, xg.at[y, own_tile], local_sem.at[0])
    fetch_dy = pltpu.make_async_copy(dy_in, dyg.at[y, own_tile], local_sem.at[1])
    fetch_wu = pltpu.make_async_copy(wu_in, wu, local_sem.at[2])
    fetch_wd = pltpu.make_async_copy(wd_in, wd, local_sem.at[3])
    for copy in (fetch_x, fetch_dy, fetch_wu, fetch_wd):
        copy.start()

    barrier = pltpu.get_barrier_semaphore()
    others = (z_up, z_down, far, y_up, y_down, near, sibling)
    for device in others:
        pl.semaphore_signal(barrier, inc=1, device_id=device, device_id_type=pl.DeviceIdType.MESH)
    pl.semaphore_wait(barrier, len(others))

    y_long, y_short = ny // 2, ny - 1 - ny // 2
    z_long, z_short = nz // 2, nz - 1 - nz // 2
    y_steps, z_steps = ny - 1, nz - 1

    def near_copy(i, ref, rows):
        return remote(ref.at[y, rows], ref.at[y, rows], xlo_s.at[i], xlo_r.at[i], near)

    fetch_x.wait()
    start(near_copy(0, xg, own_tile))
    fetch_dy.wait()
    start(near_copy(1, dyg, own_tile))

    def token_gather(i, ref, ups, downs):
        ring = Gather(
            y, ny, y_up, y_down, ups, downs,
            y_s.at[pl.ds(i * y_steps, y_steps)], y_r.at[pl.ds(i * y_steps, y_steps)], sent,
        )
        view = lambda q: ref.at[q, mine]

        def share(q):
            start(remote(ref.at[q, mine], ref.at[q, mine], sib_s.at[i, q], sib_r.at[i, q], sibling))

        def shared(q):
            remote(ref.at[q, theirs], ref.at[q, theirs], sib_s.at[i, q], sib_r.at[i, q], sibling).wait_recv()

        return ring, view, share, shared

    def token_step(gather, step, matmul):
        ring, view, share, shared = gather
        if step == 0:
            here = [y]
        else:
            here = ring.arrive(step - 1, view)
        ring.send(step, view)
        for q in here:
            share(q)
        for q in here:
            shared(q)
            matmul(q)

    def pre_chunk(q):
        pre_p[q] = dot_plain(xg[q], wu[...])

    def gact_chunk(q):
        gact_p[q] = dot_right_t(dyg[q], wd[...])

    x_gather = token_gather(0, xg, y_long, y_short)
    dy_gather = token_gather(1, dyg, y_short, y_long)

    near_copy(0, xg, near_tile).wait_recv()
    fetch_wu.wait()
    for step in range(y_long + 1):
        token_step(x_gather, step, pre_chunk)

    def z_ring(kind, i, ups, downs):
        return kind(
            z, nz, z_up, z_down, ups, downs,
            z_s.at[pl.ds(i * z_steps, z_steps)], z_r.at[pl.ds(i * z_steps, z_steps)], sent,
        )

    pre_ring = z_ring(Scatter, 0, z_long, z_short).bind(lambda q: pre_p[q], pre_out, pre_in)
    gact_ring = z_ring(Scatter, 1, z_short, z_long).bind(lambda q: gact_p[q], gact_out, gact_in)
    act_ring = z_ring(Gather, 2, z_short, z_long)
    gpre_ring = z_ring(Gather, 3, z_long, z_short)

    def pair_copy(i):
        return remote(pair_out.at[i], pair_in.at[i], pair_s.at[i], pair_r.at[i], far)

    near_copy(1, dyg, near_tile).wait_recv()
    fetch_wd.wait()
    for step in range(max(z_long, y_long + 1)):
        if step < z_long:
            pre_ring.step(step)
        if step < y_long + 1:
            token_step(dy_gather, step, gact_chunk)
    pre = pre_ring.finish()
    pre_p[z] = pre
    pair_out[0] = pre.astype(bf16)
    start(pair_copy(0))

    act_view = lambda q: act.at[q]
    gpre_view = lambda q: gpre.at[q]

    def activate():
        pair_copy(0).wait_recv()
        u = pre_p[z] + pair_in[0].astype(f32)
        t = jnp.tanh(slope_c * (u + cubic_a * u * u * u))
        act[z] = (0.5 * u * (1.0 + t)).astype(bf16)
        slope[...] = 0.5 * (1.0 + t) + 0.5 * u * (1.0 - t * t) * slope_c * (
            1.0 + 3.0 * cubic_a * u * u
        )
        act_ring.send(0, act_view)

    act_done = 0
    for step in range(z_long):
        gact_ring.step(step)
        if step == 1:
            activate()
        if step > 1:
            act_ring.arrive(act_done, act_view)
            act_done += 1
            act_ring.send(act_done, act_view)
    if z_long < 2:
        activate()
    gact = gact_ring.finish()
    gact_p[z] = gact
    pair_out[1] = gact.astype(bf16)
    start(pair_copy(1))
    while act_done < z_long:
        act_ring.arrive(act_done, act_view)
        act_done += 1
        act_ring.send(act_done, act_view)
    pair_copy(1).wait_recv()
    gpre[z] = ((gact_p[z] + pair_in[1].astype(f32)) * slope[...]).astype(bf16)

    def sib_copy(q):
        return remote(sib_out.at[q], sib_in.at[q], gsib_s.at[q], gsib_r.at[q], sibling)

    def gin_chunk(q):
        gin_p[q] = dot_right_t(gpre[q], wu[...])
        sib_out[q] = gin_p[q, theirs]
        start(sib_copy(q))

    gpre_ring.send(0, gpre_view)
    gin_chunk(z)
    rows = wu.shape[0]
    tokens = nz * 4 * tile
    third = rows // 3

    def gd_block(i):
        cols = pl.ds(i * third, third)
        left = act[:, :, cols].reshape(tokens, third)
        gd[cols, :] = dot_left_t(left, dyg[...].reshape(tokens, rows)).astype(bf16)

    def gu_block(i):
        cols = pl.ds(i * third, third)
        left = xg[:, :, cols].reshape(tokens, third)
        gu[cols, :] = dot_left_t(left, gpre[...].reshape(tokens, rows)).astype(bf16)

    for step in range(z_long):
        if step < 3:
            gd_block(step)
        here = gpre_ring.arrive(step, gpre_view)
        gpre_ring.send(step + 1, gpre_view)
        for q in here:
            gin_chunk(q)
    for step in range(z_long, 3):
        gd_block(step)
    store_gd = pltpu.make_async_copy(gd, gd_out, local_sem.at[4])
    store_gd.start()

    arrived = []

    def gin_part(q):
        sib_copy(q).wait_recv()
        return gin_p[q, mine] + sib_in[q]

    gin_ring = Scatter(y, ny, y_up, y_down, y_long, y_short, gy_s, gy_r, sent).bind(gin_part, gin_o, gin_i)
    for step in range(y_long):
        gin_ring.step(step)
        if step < 3:
            gu_block(step)
    for step in range(y_long, 3):
        gu_block(step)
    store_gu = pltpu.make_async_copy(gu, gu_out, local_sem.at[5])
    store_gu.start()
    last_p = gin_ring.finish()
    gin_p[y, mine] = last_p
    ours = pl.ds(pl.multiple_of(core * (2 * tile) + x_lo * tile, tile), tile)
    away = pl.ds(pl.multiple_of(core * (2 * tile) + (1 - x_lo) * tile, tile), tile)
    last_out[...] = gin_p[y, away]
    last = remote(last_out, last_in, gx_s.at[0], gx_r.at[0], near)
    start(last)
    last.wait_recv()
    gin_out[...] = (gin_p[y, ours] + last_in[...]).astype(bf16)
    store_gd.wait()
    store_gu.wait()
    for copy in sent:
        copy.wait_send()


def solution(mesh):
    nz = mesh.shape["row"] // 2
    ny = mesh.shape["col"] // 2

    def per_device(tokens, w_up, w_down, grad_out):
        depth, hidden = w_up.shape
        chunk = 4 * tile
        any_space = pl.BlockSpec(memory_space=pl.ANY)
        vmem_space = pl.BlockSpec(memory_space=pltpu.VMEM)
        dma = pltpu.SemaphoreType.DMA
        ys, zs = ny - 1, nz - 1
        scratch = [
            pltpu.VMEM((ny, chunk, depth), bf16),
            pltpu.VMEM((ny, chunk, depth), bf16),
            pltpu.VMEM((depth, hidden), bf16),
            pltpu.VMEM((hidden, depth), bf16),
            pltpu.VMEM((nz, chunk, hidden), f32),
            pltpu.VMEM((nz, chunk, hidden), f32),
            pltpu.VMEM((zs, chunk, hidden), bf16),
            pltpu.VMEM((zs, chunk, hidden), bf16),
            pltpu.VMEM((zs, chunk, hidden), bf16),
            pltpu.VMEM((zs, chunk, hidden), bf16),
            pltpu.VMEM((2, chunk, hidden), bf16),
            pltpu.VMEM((2, chunk, hidden), bf16),
            pltpu.VMEM((chunk, hidden), f32),
            pltpu.VMEM((nz, chunk, hidden), bf16),
            pltpu.VMEM((nz, chunk, hidden), bf16),
            pltpu.VMEM((nz, chunk, depth), f32),
            pltpu.VMEM((ny, 2 * tile, depth), f32),
            pltpu.VMEM((ny, 2 * tile, depth), f32),
            pltpu.VMEM((ys, 2 * tile, depth), f32),
            pltpu.VMEM((ys, 2 * tile, depth), f32),
            pltpu.VMEM((tile, depth), f32),
            pltpu.VMEM((tile, depth), f32),
            pltpu.VMEM((depth, hidden), bf16),
            pltpu.VMEM((hidden, depth), bf16),
            dma((6,)),
            dma((2,)), dma((2,)),
            dma((2 * ys,)), dma((2 * ys,)),
            dma((2, ny)), dma((2, ny)),
            dma((4 * zs,)), dma((4 * zs,)),
            dma((2,)), dma((2,)),
            dma((ny,)), dma((ny,)),
            dma((ys,)), dma((ys,)),
            dma((1,)), dma((1,)),
        ]
        return pl.pallas_call(
            functools.partial(kernel, nz, ny),
            out_shape=(
                jax.ShapeDtypeStruct(tokens.shape, bf16),
                jax.ShapeDtypeStruct(w_up.shape, bf16),
                jax.ShapeDtypeStruct(w_down.shape, bf16),
            ),
            in_specs=[any_space] * 4,
            out_specs=(vmem_space, any_space, any_space),
            scratch_shapes=scratch,
            compiler_params=pltpu.CompilerParams(
                collective_id=0, has_side_effects=True, vmem_limit_bytes=48 * 1024 * 1024
            ),
            cost_estimate=pl.CostEstimate(
                flops=5 * 2 * 512 * 768 * 768, bytes_accessed=5_000_000, transcendentals=64 * 768
            ),
        )(tokens, w_up, w_down, grad_out)

    in_specs = (
        P(("dp", "col"), "row"),
        P("row", ("dp", "col")),
        P(("dp", "col"), "row"),
        P(("dp", "col"), "row"),
    )
    out_specs = (P(("dp", "col"), "row"), P("row", ("dp", "col")), P(("dp", "col"), "row"))
    return jax.shard_map(
        per_device, mesh=mesh, in_specs=in_specs, out_specs=out_specs, check_vma=False
    )
```

time: 687 us -> 119 us (0.17)
  the two profiles are of different devices: /device:TPU:6 before, /device:TPU:10 now
where the time goes in v1:
time: 119 us
  Pallas kernels  112 us (94%)
  local copies, waits for them, and re-layouts  6.64 us (6%)
    pallas_call x1, Pallas kernels, per_device(): pl.pallas_call(functools.partial(kernel, nz, ny), out_shape=(jax.ShapeDty...  112 us
    unnamed x11, local copies, waits for them, and re-layouts  6.64 us

profile of v1, /device:TPU:10, one launch (start us, length us, event | category | flops | bytes accessed | tf_op | source)
XLA Modules:
  0.0 119.1 jit_solution(14028449445520014447)
XLA Ops:
  0.6 0.0 copy-start
  0.6 1.3 %copy-done = bf16[768,768]{1,0:T(8,128)(2,1)S(1)} copy-done((bf16[768,768]{1,0:T(8,128)(2,1)S(1)}, bf16[768,768]{1,0:T(8,128)(2,1)}, u32[]{:S(2)}) %copy-start) | copy-done | bytes 1179672
  1.9 0.0 copy-start.1
  1.9 1.3 %copy-done.1 = bf16[768,768]{1,0:T(8,128)(2,1)S(1)} copy-done((bf16[768,768]{1,0:T(8,128)(2,1)S(1)}, bf16[768,768]{1,0:T(8,128)(2,1)}, u32[]{:S(2)}) %copy-start.1) | copy-done | bytes 1179672
  3.2 0.0 copy-start.2
  3.2 0.7 copy-done.2
  3.9 0.0 copy-start.3
  3.9 0.7 copy-done.3
  4.6 111.8 %shard_map.67 = (bf16[16,768]{1,0:T(8,128)(2,1)S(1)}, bf16[768,768]{1,0:T(8,128)(2,1)S(1)}, bf16[768,768]{1,0:T(8,128)(2,1)S(1)}) custom-call(bf16[16,768]{1,0:T(8,128)(2,1)S(1)} %copy-done.2, bf16[768,768]{1,0:T(8,128)(2,1)S(1)} %copy-done, bf16[768,768]{1,0:T(8,128)(2,1)S(1)} %copy-done.1, bf16[16,768]{1,0:T(8,128)(2,1)S(1)} %copy-done.3), custom_call_target="tpu_custom_call" | custom-call | flops 3019898880 | bytes 5000000 | tf_op jit(solution)/shard_map/pallas_call | solution.py:389
  116.5 0.6 copy.10
  117.1 1.0 copy.11
  118.1 1.0 copy.12
Async XLA Ops:
  0.6 1.3 %copy-start = (bf16[768,768]{1,0:T(8,128)(2,1)S(1)}, bf16[768,768]{1,0:T(8,128)(2,1)}, u32[]{:S(2)}) copy-start(bf16[768,768]{1,0:T(8,128)(2,1)} %wu_in.1) | copy-start | bytes 3538948
  1.9 1.3 %copy-start.1 = (bf16[768,768]{1,0:T(8,128)(2,1)S(1)}, bf16[768,768]{1,0:T(8,128)(2,1)}, u32[]{:S(2)}) copy-start(bf16[768,768]{1,0:T(8,128)(2,1)} %wd_in.1) | copy-start | bytes 3538948
  3.2 0.7 copy-start.2
  3.9 0.7 copy-start.3

commit v2 on v1

v2 whole, which is shorter than its diff:
```python
import functools
import math

import jax
import jax.numpy as jnp
from jax import lax
from jax.experimental import pallas as pl
from jax.experimental.pallas import tpu as pltpu
from jax.sharding import PartitionSpec as P

slope_c = math.sqrt(2.0 / math.pi)
cubic_a = 0.044715
f32 = jnp.float32
bf16 = jnp.bfloat16
tile = 16


def dot_plain(left, right):
    return lax.dot_general(left, right, (((1,), (0,)), ((), ())), preferred_element_type=f32)


def dot_right_t(left, right):
    return lax.dot_general(left, right, (((1,), (1,)), ((), ())), preferred_element_type=f32)


def dot_left_t(left, right):
    return lax.dot_general(left, right, (((0,), (0,)), ((), ())), preferred_element_type=f32)


def remote(src, dst, send_sem, recv_sem, device):
    return pltpu.make_async_remote_copy(
        src_ref=src,
        dst_ref=dst,
        send_sem=send_sem,
        recv_sem=recv_sem,
        device_id=device,
        device_id_type=pl.DeviceIdType.MESH,
    )


class Ring:
    def __init__(self, place, size, up, down, ups, downs, send_sems, recv_sems, sent):
        self.place, self.size, self.sent = place, size, sent
        self.ways = ((1, ups, 0, up), (-1, downs, ups, down))
        self.send_sems, self.recv_sems = send_sems, recv_sems

    def at(self, offset):
        return lax.rem(self.place + (offset + self.size), self.size)


class Gather(Ring):
    def copy(self, way, step, view, received=False):
        sign, _, base, device = way
        q = self.at(-sign * (step + 1 if received else step))
        ref = view(q)
        slot = base + step
        return remote(ref, ref, self.send_sems.at[slot], self.recv_sems.at[slot], device)

    def send(self, step, view):
        for way in self.ways:
            if step < way[1]:
                copy = self.copy(way, step, view)
                copy.start()
                self.sent.append(copy)

    def arrive(self, step, view):
        here = []
        for way in self.ways:
            if step < way[1]:
                self.copy(way, step, view, received=True).wait_recv()
                here.append(self.at(-way[0] * (step + 1)))
        return here


class Scatter(Ring):
    def bind(self, part, out_slots, in_slots):
        self.part, self.out_slots, self.in_slots = part, out_slots, in_slots
        return self

    def copy(self, way, step):
        _, _, base, device = way
        slot = base + step
        return remote(
            self.out_slots.at[slot],
            self.in_slots.at[slot],
            self.send_sems.at[slot],
            self.recv_sems.at[slot],
            device,
        )

    def step(self, step):
        for way in self.ways:
            sign, hops, base, _ = way
            if step < hops:
                total = self.part(self.at(sign * (hops - step)))
                if step > 0:
                    self.copy(way, step - 1).wait_recv()
                    total = total + self.in_slots[base + step - 1].astype(f32)
                self.out_slots[base + step] = total.astype(self.out_slots.dtype)
                copy = self.copy(way, step)
                copy.start()
                self.sent.append(copy)

    def finish(self):
        total = self.part(self.place)
        for way in self.ways:
            _, hops, base, _ = way
            if hops > 0:
                self.copy(way, hops - 1).wait_recv()
                total = total + self.in_slots[base + hops - 1].astype(f32)
        return total


def kernel(
    nz, ny,
    x_in, wu_in, wd_in, dy_in,
    gin_out, gu, gd,
    xg, dyg, wu, wd, pre_p, gact_p,
    pre_out, pre_in, gact_out, gact_in,
    pair_out, pair_in, slope,
    act, gpre, gin_p, sib_in, near_in, last_in,
    local_sem, y_s, y_r, near_s, near_r, sib_s, sib_r, z_s, z_r, pair_s, pair_r,
    gsib_s, gsib_r, gnear_s, gnear_r, gy_s, gy_r,
):
    core = lax.axis_index("dp")
    row = lax.axis_index("row")
    col = lax.axis_index("col")
    z, x_hi = lax.div(row, 2), lax.rem(row, 2)
    x_lo, y = lax.div(col, ny), lax.rem(col, ny)
    sent = []

    def start(copy):
        copy.start()
        sent.append(copy)

    def y_peer(q):
        return {"col": x_lo * ny + q}

    def y_at(offset):
        return lax.rem(y + (offset + ny), ny)

    z_up = {"row": lax.rem(z + 1, nz) * 2 + x_hi}
    z_down = {"row": lax.rem(z + nz - 1, nz) * 2 + x_hi}
    far = {"row": z * 2 + (1 - x_hi)}
    near = {"col": (1 - x_lo) * ny + y}
    sibling = {"dp": 1 - core}

    mine = pl.ds(pl.multiple_of(core * (2 * tile), 2 * tile), 2 * tile)
    theirs = pl.ds(pl.multiple_of((1 - core) * (2 * tile), 2 * tile), 2 * tile)
    own_tile = pl.ds(pl.multiple_of(core * (2 * tile) + x_lo * tile, tile), tile)
    near_tile = pl.ds(pl.multiple_of(core * (2 * tile) + (1 - x_lo) * tile, tile), tile)

    fetch_x = pltpu.make_async_copy(x_in, xg.at[y, own_tile], local_sem.at[0])
    fetch_dy = pltpu.make_async_copy(dy_in, dyg.at[y, own_tile], local_sem.at[1])
    fetch_wu = pltpu.make_async_copy(wu_in, wu, local_sem.at[2])
    fetch_wd = pltpu.make_async_copy(wd_in, wd, local_sem.at[3])
    for copy in (fetch_x, fetch_dy, fetch_wu, fetch_wd):
        copy.start()

    barrier = pltpu.get_barrier_semaphore()
    others = [y_peer(y_at(d)) for d in range(1, ny)] + [near, z_up, z_down, far, sibling]
    for device in others:
        pl.semaphore_signal(barrier, inc=1, device_id=device, device_id_type=pl.DeviceIdType.MESH)
    pl.semaphore_wait(barrier, len(others))

    z_long, z_short = nz // 2, nz - 1 - nz // 2
    z_steps = nz - 1
    order = sorted(range(1, ny), key=lambda d: min(d, ny - d))

    def tile_copy(i, ref, d, q, device):
        view = ref.at[q, own_tile]
        return remote(view, view, y_s.at[i, d], y_r.at[i, d], device)

    def near_copy(i, ref, d, rows):
        view = ref.at[y_at(-d), rows]
        return remote(view, view, near_s.at[i, d], near_r.at[i, d], near)

    def core_copy(i, ref, d, rows):
        view = ref.at[y_at(-d), rows]
        return remote(view, view, sib_s.at[i, d], sib_r.at[i, d], sibling)

    def scatter_tile(i, ref):
        for d in reversed(order):
            start(tile_copy(i, ref, d, y, y_peer(y_at(d))))
        start(near_copy(i, ref, 0, own_tile))

    def pass_near(i, ref):
        for d in order:
            tile_copy(i, ref, d, y_at(-d), y_peer(y_at(d))).wait_recv()
            start(near_copy(i, ref, d, own_tile))

    def groups():
        steps = [[0]]
        for k in range(0, len(order), 2):
            steps.append(order[k : k + 2])
        return steps

    def pass_core(i, ref, ds):
        for d in ds:
            near_copy(i, ref, d, near_tile).wait_recv()
            start(core_copy(i, ref, d, mine))

    def multiply(i, ref, ds, dot, weights, out):
        for d in ds:
            core_copy(i, ref, d, theirs).wait_recv()
        left = [ref[y_at(-d)] for d in ds]
        left = left[0] if len(left) == 1 else jnp.concatenate(left, axis=0)
        product = dot(left, weights[...])
        for k, d in enumerate(ds):
            out[y_at(-d)] = product[k * 4 * tile : (k + 1) * 4 * tile]

    def spread(i, ref, dot, weights, out):
        before = None
        for ds in groups():
            pass_core(i, ref, ds)
            if before is not None:
                multiply(i, ref, before, dot, weights, out)
            before = ds
        multiply(i, ref, before, dot, weights, out)

    fetch_x.wait()
    scatter_tile(0, xg)
    fetch_dy.wait()
    scatter_tile(1, dyg)
    pass_near(0, xg)
    fetch_wu.wait()
    spread(0, xg, dot_plain, wu, pre_p)

    def z_ring(kind, i, ups, downs):
        return kind(
            z, nz, z_up, z_down, ups, downs,
            z_s.at[pl.ds(i * z_steps, z_steps)], z_r.at[pl.ds(i * z_steps, z_steps)], sent,
        )

    pre_ring = z_ring(Scatter, 0, z_long, z_short).bind(lambda q: pre_p[q], pre_out, pre_in)
    gact_ring = z_ring(Scatter, 1, z_short, z_long).bind(lambda q: gact_p[q], gact_out, gact_in)
    act_ring = z_ring(Gather, 2, z_short, z_long)
    gpre_ring = z_ring(Gather, 3, z_long, z_short)

    def pair_copy(i):
        return remote(pair_out.at[i], pair_in.at[i], pair_s.at[i], pair_r.at[i], far)

    pre_ring.step(0)
    pass_near(1, dyg)
    fetch_wd.wait()
    spread(1, dyg, dot_right_t, wd, gact_p)
    gact_ring.step(0)
    for step in range(1, z_long):
        pre_ring.step(step)
        gact_ring.step(step)
    pre = pre_ring.finish()
    pre_p[z] = pre
    pair_out[0] = pre.astype(bf16)
    start(pair_copy(0))
    gact = gact_ring.finish()
    gact_p[z] = gact
    pair_out[1] = gact.astype(bf16)
    start(pair_copy(1))

    act_view = lambda q: act.at[q]
    gpre_view = lambda q: gpre.at[q]
    pair_copy(0).wait_recv()
    u = pre_p[z] + pair_in[0].astype(f32)
    t = jnp.tanh(slope_c * (u + cubic_a * u * u * u))
    act[z] = (0.5 * u * (1.0 + t)).astype(bf16)
    act_ring.send(0, act_view)
    slope[...] = 0.5 * (1.0 + t) + 0.5 * u * (1.0 - t * t) * slope_c * (1.0 + 3.0 * cubic_a * u * u)
    pair_copy(1).wait_recv()
    gpre[z] = ((gact_p[z] + pair_in[1].astype(f32)) * slope[...]).astype(bf16)
    gpre_ring.send(0, gpre_view)

    def gin_core(q, rows):
        return remote(gin_p.at[q, rows], sib_in.at[q], gsib_s.at[q], gsib_r.at[q], sibling)

    def gin_near(q):
        return remote(gin_p.at[q, near_tile], near_in.at[q], gnear_s.at[q], gnear_r.at[q], near)

    def gin_owner(q, d):
        return remote(gin_p.at[q, own_tile], last_in.at[d], gy_s.at[d], gy_r.at[d], y_peer(q))

    def gin_first(q):
        gin_p[q] = dot_right_t(gpre[q], wu[...])
        start(gin_core(q, theirs))

    def gin_second(q):
        gin_core(q, theirs).wait_recv()
        gin_p[q, mine] = gin_p[q, mine] + sib_in[q]
        start(gin_near(q))

    def gin_third(q):
        gin_near(q).wait_recv()
        gin_p[q, own_tile] = gin_p[q, own_tile] + near_in[q]

        @pl.when(q != y)
        def _():
            gin_owner(q, lax.rem(q - y + ny, ny)).start()

    depth = wu.shape[0]
    tokens = nz * 4 * tile
    third = depth // 3

    def weight_block(i, left, right, out):
        cols = pl.ds(i * third, third)
        block = dot_left_t(left[:, :, cols].reshape(tokens, third), right[...].reshape(tokens, depth))
        out[cols, :] = block.astype(bf16)

    gin_first(z)
    one, two = [z], []
    for step in range(z_long):
        here = gpre_ring.arrive(step, gpre_view)
        gpre_ring.send(step + 1, gpre_view)
        act_ring.arrive(step, act_view)
        act_ring.send(step + 1, act_view)
        for q in one:
            gin_second(q)
        for q in here:
            gin_first(q)
        for q in two:
            gin_third(q)
        one, two = here, one
    weight_block(0, act, dyg, gd)
    for q in one:
        gin_second(q)
    for q in two:
        gin_third(q)
    weight_block(1, act, dyg, gd)
    weight_block(2, act, dyg, gd)
    weight_block(0, xg, gpre, gu)
    for q in one:
        gin_third(q)
    weight_block(1, xg, gpre, gu)
    weight_block(2, xg, gpre, gu)
    total = gin_p[y, own_tile]
    for d in order:
        gin_owner(y_at(d), d).wait_recv()
        total = total + last_in[d]
    gin_out[...] = total.astype(bf16)
    for d in order:
        gin_owner(y_at(d), d).wait_send()
    for copy in sent:
        copy.wait_send()


def solution(mesh):
    nz = mesh.shape["row"] // 2
    ny = mesh.shape["col"] // 2

    def per_device(tokens, w_up, w_down, grad_out):
        depth, hidden = w_up.shape
        chunk = 4 * tile
        hbm_space = pl.BlockSpec(memory_space=pltpu.HBM)
        vmem_space = pl.BlockSpec(memory_space=pltpu.VMEM)
        dma = pltpu.SemaphoreType.DMA
        zs = nz - 1
        scratch = [
            pltpu.VMEM((ny, chunk, depth), bf16),
            pltpu.VMEM((ny, chunk, depth), bf16),
            pltpu.VMEM((depth, hidden), bf16),
            pltpu.VMEM((hidden, depth), bf16),
            pltpu.VMEM((nz, chunk, hidden), f32),
            pltpu.VMEM((nz, chunk, hidden), f32),
            pltpu.VMEM((zs, chunk, hidden), bf16),
            pltpu.VMEM((zs, chunk, hidden), bf16),
            pltpu.VMEM((zs, chunk, hidden), bf16),
            pltpu.VMEM((zs, chunk, hidden), bf16),
            pltpu.VMEM((2, chunk, hidden), bf16),
            pltpu.VMEM((2, chunk, hidden), bf16),
            pltpu.VMEM((chunk, hidden), f32),
            pltpu.VMEM((nz, chunk, hidden), bf16),
            pltpu.VMEM((nz, chunk, hidden), bf16),
            pltpu.VMEM((nz, chunk, depth), f32),
            pltpu.VMEM((ny, 2 * tile, depth), f32),
            pltpu.VMEM((ny, tile, depth), f32),
            pltpu.VMEM((ny, tile, depth), f32),
            dma((4,)),
            dma((2, ny)), dma((2, ny)),
            dma((2, ny)), dma((2, ny)),
            dma((2, ny)), dma((2, ny)),
            dma((4 * zs,)), dma((4 * zs,)),
            dma((2,)), dma((2,)),
            dma((ny,)), dma((ny,)),
            dma((ny,)), dma((ny,)),
            dma((ny,)), dma((ny,)),
        ]
        return pl.pallas_call(
            functools.partial(kernel, nz, ny),
            out_shape=(
                pltpu.VMEM(tokens.shape, bf16),
                pltpu.VMEM(w_up.shape, bf16),
                pltpu.VMEM(w_down.shape, bf16),
            ),
            in_specs=[hbm_space] * 4,
            out_specs=(vmem_space, vmem_space, vmem_space),
            scratch_shapes=scratch,
            compiler_params=pltpu.CompilerParams(
                collective_id=0, has_side_effects=True, vmem_limit_bytes=60 * 1024 * 1024
            ),
            cost_estimate=pl.CostEstimate(
                flops=5 * 2 * 512 * 768 * 768, bytes_accessed=5_000_000, transcendentals=64 * 768
            ),
        )(tokens, w_up, w_down, grad_out)

    in_specs = (
        P(("dp", "col"), "row"),
        P("row", ("dp", "col")),
        P(("dp", "col"), "row"),
        P(("dp", "col"), "row"),
    )
    out_specs = (P(("dp", "col"), "row"), P("row", ("dp", "col")), P(("dp", "col"), "row"))
    return jax.shard_map(
        per_device, mesh=mesh, in_specs=in_specs, out_specs=out_specs, check_vma=False
    )
```

time: 119 us -> 93.3 us (0.78)
  the two profiles are of different devices: /device:TPU:10 before, /device:TPU:24 now
where the time goes in v2:
time: 93.3 us; the launch traced here: 93.2 us
  Pallas kernels  89.9 us (96%)
  local copies, waits for them, and re-layouts  2.64 us (3%)
    pallas_call x1, Pallas kernels, per_device(): pl.pallas_call(functools.partial(kernel, nz, ny), out_shape=(pltpu.VMEM(t...  89.9 us
    unnamed x3, local copies, waits for them, and re-layouts  2.64 us

profile of v2, /device:TPU:24, one launch (start us, length us, event | category | flops | bytes accessed | tf_op | source)
XLA Modules:
  0.0 93.2 jit_solution(11337934578008748310)
XLA Ops:
  0.6 89.9 %shard_map.67 = (bf16[16,768]{1,0:T(8,128)(2,1)S(1)}, bf16[768,768]{1,0:T(8,128)(2,1)S(1)}, bf16[768,768]{1,0:T(8,128)(2,1)S(1)}) custom-call(bf16[16,768]{1,0:T(8,128)(2,1)} %x_in.1, bf16[768,768]{1,0:T(8,128)(2,1)} %wu_in.1, bf16[768,768]{1,0:T(8,128)(2,1)} %wd_in.1, bf16[16,768]{1,0:T(8,128)(2,1)} %dy_in.1), custom_call_target="tpu_custom_call" | custom-call | flops 3019898880 | bytes 5000000 | tf_op jit(solution)/shard_map/pallas_call | solution.py:385
  90.6 0.6 copy.10
  91.2 1.0 %copy.11 = bf16[768,768]{1,0:T(8,128)(2,1)} copy(bf16[768,768]{1,0:T(8,128)(2,1)S(1)} %get-tuple-element.4) | data formatting | bytes 2359296
  92.2 1.0 %copy.12 = bf16[768,768]{1,0:T(8,128)(2,1)} copy(bf16[768,768]{1,0:T(8,128)(2,1)S(1)} %get-tuple-element.5) | data formatting | bytes 2359296

commit v3 on v2

v3 whole, which is shorter than its diff:
```python
import functools
import math

import jax
import jax.numpy as jnp
from jax import lax
from jax.experimental import pallas as pl
from jax.experimental.pallas import tpu as pltpu
from jax.sharding import PartitionSpec as P

slope_c = math.sqrt(2.0 / math.pi)
cubic_a = 0.044715
f32 = jnp.float32
bf16 = jnp.bfloat16
tile = 16


def dot_plain(left, right):
    return lax.dot_general(left, right, (((1,), (0,)), ((), ())), preferred_element_type=f32)


def dot_right_t(left, right):
    return lax.dot_general(left, right, (((1,), (1,)), ((), ())), preferred_element_type=f32)


def dot_left_t(left, right):
    return lax.dot_general(left, right, (((0,), (0,)), ((), ())), preferred_element_type=f32)


def remote(src, dst, send_sem, recv_sem, device):
    return pltpu.make_async_remote_copy(
        src_ref=src,
        dst_ref=dst,
        send_sem=send_sem,
        recv_sem=recv_sem,
        device_id=device,
        device_id_type=pl.DeviceIdType.MESH,
    )


class Row:
    def __init__(self, nz, z, x_hi, reach, send_sems, recv_sems, sent):
        self.nz, self.z, self.x_hi, self.reach, self.sent = nz, z, x_hi, reach, sent
        self.send_sems, self.recv_sems = send_sems, recv_sems

    def at(self, up):
        return lax.rem(self.z + (up + self.nz), self.nz)

    def side(self, other):
        return 1 - self.x_hi if other else self.x_hi

    def device(self, up, other):
        return {"row": self.at(up) * 2 + self.side(other)}

    def half(self, other):
        rows = 2 * tile
        return pl.ds(pl.multiple_of(self.side(other) * rows, rows), rows)

    def hops(self, sign):
        behind = range(self.reach[sign] - 2, 0, -1)
        return [(k, other) for k in behind for other in (1, 0)] + [(0, 1)]


class Scatter(Row):
    def bind(self, terms, rounded, middle, slots):
        self.terms, self.rounded, self.middle, self.slots = terms, rounded, middle, slots
        self.names = [("mid", s, k, o) for s in (1, -1) for k, o in self.hops(s)]
        self.names += [("end", s, 1, o) for s in (1, -1) for o in (1, 0)] + [("end", 0, 0, 1)]
        self.names += [("two", 1, 2, 0), ("two", -1, 2, 0)]
        return self

    def copy(self, name):
        kind, sign, k, other = name
        slot = self.names.index(name)
        if kind == "two":
            src = self.middle.at[0 if sign > 0 else 1]
        else:
            behind = 2 if kind == "mid" else 0
            src = self.rounded.at[self.at(-sign * (behind + k)), self.half(other)]
        return remote(
            src, self.slots.at[slot], self.send_sems.at[slot], self.recv_sems.at[slot],
            self.device(-sign * k, other),
        )

    def start(self, name):
        copy = self.copy(name)
        copy.start()
        self.sent.append(copy)

    def take(self, name):
        self.copy(name).wait_recv()
        return self.slots[self.names.index(name)].astype(f32)

    def begin(self):
        for kind in ("mid", "end"):
            for name in self.names:
                if name[0] == kind:
                    self.start(name)

    def relay(self):
        for sign in (1, -1):
            total = self.terms[self.at(-2 * sign), self.half(0)]
            for k, other in reversed(self.hops(sign)):
                total = total + self.take(("mid", sign, k, other))
            self.middle[0 if sign > 0 else 1] = total.astype(bf16)
            self.start(("two", sign, 2, 0))

    def finish(self):
        total = self.terms[self.z, self.half(0)]
        for name in self.names:
            if name[0] == "end":
                total = total + self.take(name)
        for sign in (1, -1):
            total = total + self.take(("two", sign, 2, 0))
        return total


class Gather(Row):
    def bind(self, ref):
        self.ref = ref
        self.near = [("far", 0, 0, 1)] + [("one", s, 1, o) for s in (1, -1) for o in (1, 0)]
        self.two = [("two", 1, 2, 0), ("two", -1, 2, 0)]
        self.late = [("fwd", s, k, o) for s in (1, -1) for k, o in self.hops(s)]
        self.names = self.two + self.near + self.late
        return self

    def copy(self, name, received=False):
        kind, sign, k, other = name
        slot = self.names.index(name)
        behind = 2 if kind == "fwd" else 0
        if received:
            view = self.ref.at[self.at(-sign * (behind + k)), self.half(other)]
        else:
            view = self.ref.at[self.at(-sign * behind), self.half(0)]
        return remote(
            view, view, self.send_sems.at[slot], self.recv_sems.at[slot], self.device(sign * k, other)
        )

    def start(self, name):
        copy = self.copy(name)
        copy.start()
        self.sent.append(copy)

    def begin(self):
        for name in self.two + self.near:
            self.start(name)

    def relay(self):
        for name in self.two:
            self.copy(name, received=True).wait_recv()
            for late in self.late:
                if late[1] == name[1]:
                    self.start(late)

    def arrive(self, names):
        for name in names:
            self.copy(name, received=True).wait_recv()


def kernel(
    nz, ny,
    x_in, wu_in, wd_in, dy_in,
    gin_out, gu, gd,
    xg, dyg, wu, wd, pre_p, gact_p,
    pre_b, gact_b, middle, slots, slope,
    act, gpre, gin_p, sib_in, near_o, near_in, last_o, last_in,
    local_sem, y_s, y_r, near_s, near_r, sib_s, sib_r, z_s, z_r,
    gsib_s, gsib_r, gnear_s, gnear_r, gy_s, gy_r,
):
    core = lax.axis_index("dp")
    row = lax.axis_index("row")
    col = lax.axis_index("col")
    z, x_hi = lax.div(row, 2), lax.rem(row, 2)
    x_lo, y = lax.div(col, ny), lax.rem(col, ny)
    sent = []

    def start(copy):
        copy.start()
        sent.append(copy)

    def y_peer(q):
        return {"col": x_lo * ny + q}

    def y_at(offset):
        return lax.rem(y + (offset + ny), ny)

    near = {"col": (1 - x_lo) * ny + y}
    sibling = {"dp": 1 - core}

    mine = pl.ds(pl.multiple_of(core * (2 * tile), 2 * tile), 2 * tile)
    theirs = pl.ds(pl.multiple_of((1 - core) * (2 * tile), 2 * tile), 2 * tile)
    own_tile = pl.ds(pl.multiple_of(core * (2 * tile) + x_lo * tile, tile), tile)
    near_tile = pl.ds(pl.multiple_of(core * (2 * tile) + (1 - x_lo) * tile, tile), tile)

    fetch_x = pltpu.make_async_copy(x_in, xg.at[y, own_tile], local_sem.at[0])
    fetch_dy = pltpu.make_async_copy(dy_in, dyg.at[y, own_tile], local_sem.at[1])
    fetch_wu = pltpu.make_async_copy(wu_in, wu, local_sem.at[2])
    fetch_wd = pltpu.make_async_copy(wd_in, wd, local_sem.at[3])
    for copy in (fetch_x, fetch_dy, fetch_wu, fetch_wd):
        copy.start()

    barrier = pltpu.get_barrier_semaphore()
    place = Row(nz, z, x_hi, {}, None, None, None)
    others = [y_peer(y_at(d)) for d in range(1, ny)] + [near, sibling, place.device(0, 1)]
    others += [place.device(up, other) for up in (1, -1, 2, -2) for other in (0, 1)]
    for device in others:
        pl.semaphore_signal(barrier, inc=1, device_id=device, device_id_type=pl.DeviceIdType.MESH)
    pl.semaphore_wait(barrier, len(others))

    z_long, z_short = nz // 2, nz - 1 - nz // 2
    order = sorted(range(1, ny), key=lambda d: min(d, ny - d))

    def tile_copy(i, ref, d, q, device):
        view = ref.at[q, own_tile]
        return remote(view, view, y_s.at[i, d], y_r.at[i, d], device)

    def near_copy(i, ref, d, rows):
        view = ref.at[y_at(-d), rows]
        return remote(view, view, near_s.at[i, d], near_r.at[i, d], near)

    def core_copy(i, ref, d, rows):
        view = ref.at[y_at(-d), rows]
        return remote(view, view, sib_s.at[i, d], sib_r.at[i, d], sibling)

    def scatter_tile(i, ref):
        for d in reversed(order):
            start(tile_copy(i, ref, d, y, y_peer(y_at(d))))
        start(near_copy(i, ref, 0, own_tile))

    def pass_near(i, ref):
        for d in order:
            tile_copy(i, ref, d, y_at(-d), y_peer(y_at(d))).wait_recv()
            start(near_copy(i, ref, d, own_tile))

    def groups():
        steps = [[0]]
        for k in range(0, len(order), 2):
            steps.append(order[k : k + 2])
        return steps

    def pass_core(i, ref, ds):
        for d in ds:
            near_copy(i, ref, d, near_tile).wait_recv()
            start(core_copy(i, ref, d, mine))

    def multiply(i, ref, ds, dot, weights, out, rounded):
        for d in ds:
            core_copy(i, ref, d, theirs).wait_recv()
        left = [ref[y_at(-d)] for d in ds]
        left = left[0] if len(left) == 1 else jnp.concatenate(left, axis=0)
        product = dot(left, weights[...])
        for k, d in enumerate(ds):
            block = product[k * 4 * tile : (k + 1) * 4 * tile]
            out[y_at(-d)] = block
            rounded[y_at(-d)] = block.astype(bf16)

    def spread(i, ref, dot, weights, out, rounded):
        before = None
        for ds in groups():
            pass_core(i, ref, ds)
            if before is not None:
                multiply(i, ref, before, dot, weights, out, rounded)
            before = ds
        multiply(i, ref, before, dot, weights, out, rounded)

    fetch_x.wait()
    scatter_tile(0, xg)
    fetch_dy.wait()
    scatter_tile(1, dyg)
    pass_near(0, xg)
    pass_near(1, dyg)
    fetch_wu.wait()
    spread(0, xg, dot_plain, wu, pre_p, pre_b)

    def on_row(kind, i, ups, downs):
        return kind(nz, z, x_hi, {1: ups, -1: downs}, z_s.at[i], z_r.at[i], sent)

    pre_sum = on_row(Scatter, 0, z_long, z_short).bind(pre_p, pre_b, middle.at[0], slots.at[0])
    gact_sum = on_row(Scatter, 1, z_short, z_long).bind(gact_p, gact_b, middle.at[1], slots.at[1])
    act_all = on_row(Gather, 2, z_short, z_long).bind(act)
    gpre_all = on_row(Gather, 3, z_long, z_short).bind(gpre)
    block = place.half(0)

    pre_sum.begin()
    fetch_wd.wait()
    spread(1, dyg, dot_right_t, wd, gact_p, gact_b)
    gact_sum.begin()
    pre_sum.relay()
    gact_sum.relay()
    u = pre_sum.finish()
    t = jnp.tanh(slope_c * (u + cubic_a * u * u * u))
    act[z, block] = (0.5 * u * (1.0 + t)).astype(bf16)
    slope[...] = 0.5 * (1.0 + t) + 0.5 * u * (1.0 - t * t) * slope_c * (1.0 + 3.0 * cubic_a * u * u)
    gpre[z, block] = (gact_sum.finish() * slope[...]).astype(bf16)
    gpre_all.begin()

    def gin_core(q, rows):
        return remote(gin_p.at[q, rows], sib_in.at[q], gsib_s.at[q], gsib_r.at[q], sibling)

    def gin_near(q):
        return remote(near_o.at[q], near_in.at[q], gnear_s.at[q], gnear_r.at[q], near)

    def gin_owner(q, d):
        return remote(last_o.at[q], last_in.at[d], gy_s.at[d], gy_r.at[d], y_peer(q))

    def gin_first(group):
        product = dot_right_t(jnp.concatenate([gpre[q] for q in group], axis=0), wu[...])
        for k, q in enumerate(group):
            gin_p[q] = product[k * 4 * tile : (k + 1) * 4 * tile]
            start(gin_core(q, theirs))

    def gin_second(q):
        gin_core(q, theirs).wait_recv()
        gin_p[q, mine] = gin_p[q, mine] + sib_in[q]
        near_o[q] = gin_p[q, near_tile].astype(bf16)
        start(gin_near(q))

    def gin_third(q):
        gin_near(q).wait_recv()
        total = gin_p[q, own_tile] + near_in[q].astype(f32)
        gin_p[q, own_tile] = total
        last_o[q] = total.astype(bf16)

        @pl.when(q != y)
        def _():
            gin_owner(q, lax.rem(q - y + ny, ny)).start()

    depth = wu.shape[0]
    tokens = nz * 4 * tile
    third = depth // 3

    def weight_block(i, left, right, out):
        cols = pl.ds(i * third, third)
        block = dot_left_t(left[:, :, cols].reshape(tokens, third), right[...].reshape(tokens, depth))
        out[cols, :] = block.astype(bf16)

    early = [z] + [place.at(up) for up in (1, -1)]
    late = [place.at(up) for up in (2, -2, 3, -3, 4)]
    gpre_all.relay()
    act_all.begin()
    gpre_all.arrive(gpre_all.near)
    gin_first(early)
    for q in early:
        gin_second(q)
    gpre_all.arrive(gpre_all.late)
    gin_first(late[:2])
    gin_first(late[2:])
    act_all.relay()
    for q in early:
        gin_third(q)
    for q in late:
        gin_second(q)
    weight_block(0, xg, gpre, gu)
    weight_block(1, xg, gpre, gu)
    weight_block(2, xg, gpre, gu)
    for q in late:
        gin_third(q)
    act_all.arrive(act_all.near + act_all.late)
    weight_block(0, act, dyg, gd)
    weight_block(1, act, dyg, gd)
    weight_block(2, act, dyg, gd)
    total = gin_p[y, own_tile]
    for d in order:
        gin_owner(y_at(d), d).wait_recv()
        total = total + last_in[d].astype(f32)
    gin_out[...] = total.astype(bf16)
    for d in order:
        gin_owner(y_at(d), d).wait_send()
    for copy in sent:
        copy.wait_send()


def solution(mesh):
    nz = mesh.shape["row"] // 2
    ny = mesh.shape["col"] // 2

    def per_device(tokens, w_up, w_down, grad_out):
        depth, hidden = w_up.shape
        chunk = 4 * tile
        hbm_space = pl.BlockSpec(memory_space=pltpu.HBM)
        vmem_space = pl.BlockSpec(memory_space=pltpu.VMEM)
        dma = pltpu.SemaphoreType.DMA
        scratch = [
            pltpu.VMEM((ny, chunk, depth), bf16),
            pltpu.VMEM((ny, chunk, depth), bf16),
            pltpu.VMEM((depth, hidden), bf16),
            pltpu.VMEM((hidden, depth), bf16),
            pltpu.VMEM((nz, chunk, hidden), f32),
            pltpu.VMEM((nz, chunk, hidden), f32),
            pltpu.VMEM((nz, chunk, hidden), bf16),
            pltpu.VMEM((nz, chunk, hidden), bf16),
            pltpu.VMEM((2, 2, 2 * tile, hidden), bf16),
            pltpu.VMEM((2, 2 * nz - 1, 2 * tile, hidden), bf16),
            pltpu.VMEM((2 * tile, hidden), f32),
            pltpu.VMEM((nz, chunk, hidden), bf16),
            pltpu.VMEM((nz, chunk, hidden), bf16),
            pltpu.VMEM((nz, chunk, depth), f32),
            pltpu.VMEM((ny, 2 * tile, depth), f32),
            pltpu.VMEM((ny, tile, depth), bf16),
            pltpu.VMEM((ny, tile, depth), bf16),
            pltpu.VMEM((ny, tile, depth), bf16),
            pltpu.VMEM((ny, tile, depth), bf16),
            dma((4,)),
            dma((2, ny)), dma((2, ny)),
            dma((2, ny)), dma((2, ny)),
            dma((2, ny)), dma((2, ny)),
            dma((4, 2 * nz - 1)), dma((4, 2 * nz - 1)),
            dma((ny,)), dma((ny,)),
            dma((ny,)), dma((ny,)),
            dma((ny,)), dma((ny,)),
        ]
        return pl.pallas_call(
            functools.partial(kernel, nz, ny),
            out_shape=(
                pltpu.VMEM(tokens.shape, bf16),
                pltpu.VMEM(w_up.shape, bf16),
                pltpu.VMEM(w_down.shape, bf16),
            ),
            in_specs=[hbm_space] * 4,
            out_specs=(vmem_space, vmem_space, vmem_space),
            scratch_shapes=scratch,
            compiler_params=pltpu.CompilerParams(
                collective_id=0, has_side_effects=True, vmem_limit_bytes=60 * 1024 * 1024
            ),
            cost_estimate=pl.CostEstimate(
                flops=5 * 2 * 512 * 768 * 768, bytes_accessed=5_000_000, transcendentals=64 * 768
            ),
        )(tokens, w_up, w_down, grad_out)

    in_specs = (
        P(("dp", "col"), "row"),
        P("row", ("dp", "col")),
        P(("dp", "col"), "row"),
        P(("dp", "col"), "row"),
    )
    out_specs = (P(("dp", "col"), "row"), P("row", ("dp", "col")), P(("dp", "col"), "row"))
    return jax.shard_map(
        per_device, mesh=mesh, in_specs=in_specs, out_specs=out_specs, check_vma=False
    )
```

time: 93.3 us -> 85.2 us (0.913)
  the two profiles are of different devices: /device:TPU:24 before, /device:TPU:28 now
where the time goes in v3:
time: 85.2 us; the launch traced here: 85.1 us
  Pallas kernels  81.8 us (96%)
  local copies, waits for them, and re-layouts  2.64 us (3%)
    pallas_call x1, Pallas kernels, per_device(): pl.pallas_call(functools.partial(kernel, nz, ny), out_shape=(pltpu.VMEM(t...  81.8 us
    unnamed x3, local copies, waits for them, and re-layouts  2.64 us

profile of v3, /device:TPU:28, one launch (start us, length us, event | category | flops | bytes accessed | tf_op | source)
XLA Modules:
  0.0 85.1 jit_solution(15275291822383141106)
XLA Ops:
  0.6 81.8 %shard_map.67 = (bf16[16,768]{1,0:T(8,128)(2,1)S(1)}, bf16[768,768]{1,0:T(8,128)(2,1)S(1)}, bf16[768,768]{1,0:T(8,128)(2,1)S(1)}) custom-call(bf16[16,768]{1,0:T(8,128)(2,1)} %x_in.1, bf16[768,768]{1,0:T(8,128)(2,1)} %wu_in.1, bf16[768,768]{1,0:T(8,128)(2,1)} %wd_in.1, bf16[16,768]{1,0:T(8,128)(2,1)} %dy_in.1), custom_call_target="tpu_custom_call" | custom-call | flops 3019898880 | bytes 5000000 | tf_op jit(solution)/shard_map/pallas_call | solution.py:412
  82.5 0.6 copy.10
  83.1 1.0 %copy.11 = bf16[768,768]{1,0:T(8,128)(2,1)} copy(bf16[768,768]{1,0:T(8,128)(2,1)S(1)} %get-tuple-element.4) | data formatting | bytes 2359296
  84.1 1.0 %copy.12 = bf16[768,768]{1,0:T(8,128)(2,1)} copy(bf16[768,768]{1,0:T(8,128)(2,1)S(1)} %get-tuple-element.5) | data formatting | bytes 2359296

commit v4 on v3

--- a/solution.py
+++ b/solution.py
@@ -17,10 +17,6 @@
 
 def dot_plain(left, right):
     return lax.dot_general(left, right, (((1,), (0,)), ((), ())), preferred_element_type=f32)
-
-
-def dot_right_t(left, right):
-    return lax.dot_general(left, right, (((1,), (1,)), ((), ())), preferred_element_type=f32)
 
 
 def dot_left_t(left, right):
@@ -92,10 +88,14 @@
         return self.slots[self.names.index(name)].astype(f32)
 
     def begin(self):
-        for kind in ("mid", "end"):
-            for name in self.names:
-                if name[0] == kind:
-                    self.start(name)
+        for name in self.names:
+            if name[0] == "mid":
+                self.start(name)
+
+    def begin_near(self):
+        for name in self.names:
+            if name[0] == "end":
+                self.start(name)
 
     def relay(self):
         for sign in (1, -1):
@@ -161,7 +161,7 @@
     nz, ny,
     x_in, wu_in, wd_in, dy_in,
     gin_out, gu, gd,
-    xg, dyg, wu, wd, pre_p, gact_p,
+    xg, dyg, wu, wd, wut, wdt, pre_p, gact_p,
     pre_b, gact_b, middle, slots, slope,
     act, gpre, gin_p, sib_in, near_o, near_in, last_o, last_in,
     local_sem, y_s, y_r, near_s, near_r, sib_s, sib_r, z_s, z_r,
@@ -233,10 +233,8 @@
             start(near_copy(i, ref, d, own_tile))
 
     def groups():
-        steps = [[0]]
-        for k in range(0, len(order), 2):
-            steps.append(order[k : k + 2])
-        return steps
+        cut = len(order) // 2 + 1
+        return [[0] + order[:cut], order[cut:]]
 
     def pass_core(i, ref, ds):
         for d in ds:
@@ -267,9 +265,12 @@
     scatter_tile(0, xg)
     fetch_dy.wait()
     scatter_tile(1, dyg)
+    fetch_wd.wait()
+    wdt[...] = wd[...].T
+    fetch_wu.wait()
+    wut[...] = wu[...].T
     pass_near(0, xg)
     pass_near(1, dyg)
-    fetch_wu.wait()
     spread(0, xg, dot_plain, wu, pre_p, pre_b)
 
     def on_row(kind, i, ups, downs):
@@ -282,11 +283,12 @@
     block = place.half(0)
 
     pre_sum.begin()
-    fetch_wd.wait()
-    spread(1, dyg, dot_right_t, wd, gact_p, gact_b)
+    spread(1, dyg, dot_plain, wdt, gact_p, gact_b)
     gact_sum.begin()
     pre_sum.relay()
+    pre_sum.begin_near()
     gact_sum.relay()
+    gact_sum.begin_near()
     u = pre_sum.finish()
     t = jnp.tanh(slope_c * (u + cubic_a * u * u * u))
     act[z, block] = (0.5 * u * (1.0 + t)).astype(bf16)
@@ -304,7 +306,7 @@
         return remote(last_o.at[q], last_in.at[d], gy_s.at[d], gy_r.at[d], y_peer(q))
 
     def gin_first(group):
-        product = dot_right_t(jnp.concatenate([gpre[q] for q in group], axis=0), wu[...])
+        product = dot_plain(jnp.concatenate([gpre[q] for q in group], axis=0), wut[...])
         for k, q in enumerate(group):
             gin_p[q] = product[k * 4 * tile : (k + 1) * 4 * tile]
             start(gin_core(q, theirs))
@@ -385,6 +387,8 @@
             pltpu.VMEM((ny, chunk, depth), bf16),
             pltpu.VMEM((depth, hidden), bf16),
             pltpu.VMEM((hidden, depth), bf16),
+            pltpu.VMEM((hidden, depth), bf16),
+            pltpu.VMEM((depth, hidden), bf16),
             pltpu.VMEM((nz, chunk, hidden), f32),
             pltpu.VMEM((nz, chunk, hidden), f32),
             pltpu.VMEM((nz, chunk, hidden), bf16),

time: 85.2 us -> 82.5 us (0.968)
  the two profiles are of different devices: /device:TPU:28 before, /device:TPU:24 now
where the time goes in v4:
time: 82.5 us; the launch traced here: 82.4 us
  Pallas kernels  79.1 us (96%)
  local copies, waits for them, and re-layouts  2.64 us (3%)
    pallas_call x1, Pallas kernels, per_device(): pl.pallas_call(functools.partial(kernel, nz, ny), out_shape=(pltpu.VMEM(t...  79.1 us
    unnamed x3, local copies, waits for them, and re-layouts  2.64 us

profile of v4, /device:TPU:24, one launch (start us, length us, event | category | flops | bytes accessed | tf_op | source)
XLA Modules:
  0.0 82.4 jit_solution(4083920571352314938)
XLA Ops:
  0.6 79.1 %shard_map.67 = (bf16[16,768]{1,0:T(8,128)(2,1)S(1)}, bf16[768,768]{1,0:T(8,128)(2,1)S(1)}, bf16[768,768]{1,0:T(8,128)(2,1)S(1)}) custom-call(bf16[16,768]{1,0:T(8,128)(2,1)} %x_in.1, bf16[768,768]{1,0:T(8,128)(2,1)} %wu_in.1, bf16[768,768]{1,0:T(8,128)(2,1)} %wd_in.1, bf16[16,768]{1,0:T(8,128)(2,1)} %dy_in.1), custom_call_target="tpu_custom_call" | custom-call | flops 3019898880 | bytes 5000000 | tf_op jit(solution)/shard_map/pallas_call | solution.py:416
  79.7 0.6 copy.10
  80.3 1.0 %copy.11 = bf16[768,768]{1,0:T(8,128)(2,1)} copy(bf16[768,768]{1,0:T(8,128)(2,1)S(1)} %get-tuple-element.4) | data formatting | bytes 2359296
  81.3 1.0 %copy.12 = bf16[768,768]{1,0:T(8,128)(2,1)} copy(bf16[768,768]{1,0:T(8,128)(2,1)S(1)} %get-tuple-element.5) | data formatting | bytes 2359296

commit v5 on v4

--- a/solution.py
+++ b/solution.py
@@ -347,11 +347,11 @@
     gpre_all.arrive(gpre_all.late)
     gin_first(late[:2])
     gin_first(late[2:])
-    act_all.relay()
+    for q in late:
+        gin_second(q)
     for q in early:
         gin_third(q)
-    for q in late:
-        gin_second(q)
+    act_all.relay()
     weight_block(0, xg, gpre, gu)
     weight_block(1, xg, gpre, gu)
     weight_block(2, xg, gpre, gu)

time: 82.5 us -> 84 us (1.018)
  the two profiles are of different devices: /device:TPU:24 before, /device:TPU:1 now
where the time goes in v5:
time: 84 us; the launch traced here: 83.9 us
  Pallas kernels  80.6 us (96%)
  local copies, waits for them, and re-layouts  2.64 us (3%)
    pallas_call x1, Pallas kernels, per_device(): pl.pallas_call(functools.partial(kernel, nz, ny), out_shape=(pltpu.VMEM(t...  80.6 us
    unnamed x3, local copies, waits for them, and re-layouts  2.64 us

profile of v5, /device:TPU:1, one launch (start us, length us, event | category | flops | bytes accessed | tf_op | source)
XLA Modules:
  0.0 83.9 jit_solution(5714081687079383493)
XLA Ops:
  0.6 80.6 %shard_map.67 = (bf16[16,768]{1,0:T(8,128)(2,1)S(1)}, bf16[768,768]{1,0:T(8,128)(2,1)S(1)}, bf16[768,768]{1,0:T(8,128)(2,1)S(1)}) custom-call(bf16[16,768]{1,0:T(8,128)(2,1)} %x_in.1, bf16[768,768]{1,0:T(8,128)(2,1)} %wu_in.1, bf16[768,768]{1,0:T(8,128)(2,1)} %wd_in.1, bf16[16,768]{1,0:T(8,128)(2,1)} %dy_in.1), custom_call_target="tpu_custom_call" | custom-call | flops 3019898880 | bytes 5000000 | tf_op jit(solution)/shard_map/pallas_call | solution.py:416
  81.3 0.6 copy.10
  81.9 1.0 %copy.11 = bf16[768,768]{1,0:T(8,128)(2,1)} copy(bf16[768,768]{1,0:T(8,128)(2,1)S(1)} %get-tuple-element.4) | data formatting | bytes 2359296
  82.9 1.0 %copy.12 = bf16[768,768]{1,0:T(8,128)(2,1)} copy(bf16[768,768]{1,0:T(8,128)(2,1)S(1)} %get-tuple-element.5) | data formatting | bytes 2359296
